TPU v7x, 32 devices: a whole 2x2x4 slice. The times are simulated.
32 devices in a mesh: replica: 4 (over x, core), shard: 8 (over z, y).
Axes of the slice: x: 2, y: 2, z: 4, core: 2. Of those that a mesh axis runs over, the one named last changes fastest.
Arguments:
- tokens: bfloat16 [32768, 768], P(('replica', 'shard')), may hold values from -6 to 6
- gain_attn: bfloat16 [768], P('shard'), may hold values from 0.099609375 to 1.8984375
- w_qkv: bfloat16 [768, 2304], P('shard'), may hold values from -0.3125 to 0.3125
- w_out: bfloat16 [768, 768], P('shard'), may hold values from -0.875 to 0.875
- gain_ffn: bfloat16 [768], P('shard'), may hold values from 0.099609375 to 1.8984375
- w_in: bfloat16 [768, 2304], P('shard'), may hold values from -0.21875 to 0.21875
- w_down: bfloat16 [1152, 768], P('shard'), may hold values from -0.1875 to 0.1875
- cotangent: bfloat16 [32768, 768], P(('replica', 'shard')), may hold values from -6 to 6
Outputs:
- output: bfloat16 [32768, 768], P(('replica', 'shard'))
- input_grad: bfloat16 [32768, 768], P(('replica', 'shard'))
- grad_gain_attn: float32 [768], P('shard')
- grad_qkv: float32 [768, 2304], P('shard')
- grad_out: float32 [768, 768], P('shard')
- grad_gain_ffn: float32 [768], P('shard')
- grad_in: float32 [768, 2304], P('shard')
- grad_down: float32 [1152, 768], P('shard')
All inputs are finite; a program needn't handle non-finite values.
Results may differ from a plain program's by a relative error of at most 0.018.
Values may be sent and summed in bfloat16 or wider, within the bound.
A program may use at most 128 MiB of HBM per device.

v0:
```python
import math
import jax
import jax.numpy as jnp
from jax import lax
from jax.sharding import PartitionSpec as P

D = 768
HEADS = 12
HEAD_DIM = 64
FF = 1152
WINDOW = 128
LENGTH = 1024
epsilon = 1e-05


def normalize(values):
    centre = values - jnp.mean(values, axis=-1, keepdims=True)
    inverse = lax.rsqrt(jnp.mean(centre * centre, axis=-1, keepdims=True) + epsilon)
    return (centre * inverse, inverse)


def norm_back(grad_norm, standard, inverse, gain):
    scaled = grad_norm * gain
    return inverse * (
        scaled
        - jnp.mean(scaled, axis=-1, keepdims=True)
        - standard * jnp.mean(scaled * standard, axis=-1, keepdims=True)
    )


def rotary_tables(count):
    half_dim = HEAD_DIM // 2
    freqs = 10000.0 ** (-(jnp.arange(half_dim, dtype=jnp.float32) * 2.0) / HEAD_DIM)
    places = (jnp.arange(count, dtype=jnp.int32) % LENGTH).astype(jnp.float32)
    angles = places[:, None] * freqs[None, :]
    angles = jnp.concatenate([angles, angles], axis=1)
    return (jnp.cos(angles)[:, None, :], jnp.sin(angles)[:, None, :])


def rotate_half(values):
    half_dim = values.shape[-1] // 2
    return jnp.concatenate([-values[..., half_dim:], values[..., :half_dim]], axis=-1)


def rotate_back(values):
    half_dim = values.shape[-1] // 2
    return jnp.concatenate([values[..., half_dim:], -values[..., :half_dim]], axis=-1)


def windows(field, block_rows, margin):
    seq_count = field.shape[0] // LENGTH
    blocks = LENGTH // block_rows
    shaped = field.reshape(seq_count, LENGTH, HEADS, HEAD_DIM)
    padded = jnp.pad(shaped, ((0, 0), (margin, block_rows - margin), (0, 0), (0, 0)))
    first = padded[:, :LENGTH].reshape(seq_count, blocks, block_rows, HEADS, HEAD_DIM)
    second = padded[:, block_rows : block_rows + LENGTH].reshape(
        seq_count, blocks, block_rows, HEADS, HEAD_DIM
    )
    joined = jnp.concatenate([first, second[:, :, : 2 * margin]], axis=2)
    return joined.reshape(seq_count * blocks, block_rows + 2 * margin, HEADS, HEAD_DIM)


def unwindow(field, block_rows, margin):
    blocks = LENGTH // block_rows
    seq_count = field.shape[0] // blocks
    shaped = field.reshape(seq_count, blocks, block_rows + 2 * margin, HEADS, HEAD_DIM)
    first = shaped[:, :, :block_rows].reshape(seq_count, LENGTH, HEADS, HEAD_DIM)
    second = jnp.pad(
        shaped[:, :, block_rows:], ((0, 0), (0, 0), (0, block_rows - 2 * margin), (0, 0), (0, 0))
    )
    second = second.reshape(seq_count, LENGTH, HEADS, HEAD_DIM)
    whole = jnp.pad(first, ((0, 0), (0, block_rows), (0, 0), (0, 0))) + jnp.pad(
        second, ((0, 0), (block_rows, 0), (0, 0), (0, 0))
    )
    return whole[:, margin : margin + LENGTH].reshape(seq_count * LENGTH, HEADS, HEAD_DIM)


def to_items(field):
    per_group = math.gcd(HEADS, 4)
    head_groups = HEADS // per_group
    count, rows = (field.shape[0], field.shape[1])
    shaped = field.reshape(count, rows, head_groups, per_group, HEAD_DIM).transpose(0, 2, 1, 3, 4)
    return shaped.reshape(count * head_groups, rows, per_group, HEAD_DIM)


def from_items(field):
    per_group = math.gcd(HEADS, 4)
    head_groups = HEADS // per_group
    count, rows = (field.shape[0] // head_groups, field.shape[1])
    shaped = field.reshape(count, head_groups, rows, per_group, HEAD_DIM).transpose(0, 2, 1, 3, 4)
    return shaped.reshape(count, rows, HEADS, HEAD_DIM)


def block_scores(query_part, key_part, start, block_rows, margin):
    span = key_part.shape[0]
    query_pos = start + jnp.arange(block_rows, dtype=jnp.int32)[:, None]
    key_pos = start - margin + jnp.arange(span, dtype=jnp.int32)[None, :]
    allowed = (key_pos >= 0) & (key_pos < LENGTH) & (jnp.abs(query_pos - key_pos) <= margin)
    raw = jnp.einsum(
        "qhd,khd->hqk", query_part, key_part, preferred_element_type=jnp.float32
    ) * HEAD_DIM ** (-0.5)
    return jnp.where(allowed[None], raw, -1e30)


def block_starts(count, block_rows):
    per_group = math.gcd(HEADS, 4)
    blocks = LENGTH // block_rows
    starts = jnp.arange(count, dtype=jnp.int32) % blocks * block_rows
    return jnp.repeat(starts, HEADS // per_group)


def attend_forward(queries, keys, values):
    count_tok = queries.shape[0]
    block_rows = min(512, LENGTH)
    margin = WINDOW // 2
    query_items = to_items(queries.reshape(count_tok // block_rows, block_rows, HEADS, HEAD_DIM))
    key_items = to_items(windows(keys, block_rows, margin))
    value_items = to_items(windows(values, block_rows, margin))
    starts = block_starts(count_tok // block_rows, block_rows)

    def one_block(pieces):
        query_part, key_part, value_part, start = pieces
        scores = block_scores(query_part, key_part, start, block_rows, margin)
        top = jnp.max(scores, axis=-1, keepdims=True)
        expo = jnp.exp(scores - top)
        total = jnp.sum(expo, axis=-1, keepdims=True)
        probs = (expo / total).astype(jnp.bfloat16)
        mixed = jnp.einsum("hqk,khd->qhd", probs, value_part, preferred_element_type=jnp.float32)
        return (mixed.astype(jnp.bfloat16), top[..., 0] + jnp.log(total[..., 0]))

    mixed, log_totals = lax.map(one_block, (query_items, key_items, value_items, starts))
    return (from_items(mixed).reshape(count_tok, D), log_totals)


def attend_backward(queries, keys, values, grad_mixed, log_totals):
    count_tok = queries.shape[0]
    block_rows = min(512, LENGTH)
    margin = WINDOW // 2
    scale = HEAD_DIM ** (-0.5)
    query_items = to_items(queries.reshape(count_tok // block_rows, block_rows, HEADS, HEAD_DIM))
    grad_items = to_items(grad_mixed.reshape(count_tok // block_rows, block_rows, HEADS, HEAD_DIM))
    key_items = to_items(windows(keys, block_rows, margin))
    value_items = to_items(windows(values, block_rows, margin))
    starts = block_starts(count_tok // block_rows, block_rows)

    def one_block(pieces):
        query_part, key_part, value_part, grad_part, log_part, start = pieces
        scores = block_scores(query_part, key_part, start, block_rows, margin)
        probs = jnp.exp(scores - log_part[..., None])
        grad_probs = jnp.einsum(
            "qhd,khd->hqk", grad_part, value_part, preferred_element_type=jnp.float32
        )
        centre = jnp.sum(grad_probs * probs, axis=-1, keepdims=True)
        grad_scores = (probs * (grad_probs - centre)).astype(jnp.bfloat16)
        grad_query = (
            jnp.einsum("hqk,khd->qhd", grad_scores, key_part, preferred_element_type=jnp.float32)
            * scale
        )
        grad_key = (
            jnp.einsum("hqk,qhd->khd", grad_scores, query_part, preferred_element_type=jnp.float32)
            * scale
        )
        grad_value = jnp.einsum(
            "hqk,qhd->khd",
            probs.astype(jnp.bfloat16),
            grad_part,
            preferred_element_type=jnp.float32,
        )
        return (grad_query, grad_key, grad_value)

    grad_query, grad_key, grad_value = lax.map(
        one_block, (query_items, key_items, value_items, grad_items, log_totals, starts)
    )
    grad_query = from_items(grad_query).reshape(count_tok, HEADS, HEAD_DIM)
    grad_key = unwindow(from_items(grad_key), block_rows, margin)
    grad_value = unwindow(from_items(grad_value), block_rows, margin)
    return (grad_query, grad_key, grad_value)


def body(tokens, gain_attn, w_qkv, w_out, gain_ffn, w_in, w_down, cotangent):
    count_tok = tokens.shape[0]
    gain_one, joint_weight, out_weight = (
        lax.all_gather(gain_attn, "shard", axis=0, tiled=True),
        lax.all_gather(w_qkv, "shard", axis=0, tiled=True),
        lax.all_gather(w_out, "shard", axis=0, tiled=True),
    )
    gain_two, in_weight, down_weight = (
        lax.all_gather(gain_ffn, "shard", axis=0, tiled=True),
        lax.all_gather(w_in, "shard", axis=0, tiled=True),
        lax.all_gather(w_down, "shard", axis=0, tiled=True),
    )
    stream = tokens.astype(jnp.float32)
    standard_one, inverse_one = normalize(stream)
    normed_attn = (standard_one * gain_one.astype(jnp.float32)).astype(jnp.bfloat16)
    projected = jnp.dot(normed_attn, joint_weight, preferred_element_type=jnp.float32)
    projected = projected.reshape(count_tok, 3, HEADS, HEAD_DIM)
    cosine, sine = rotary_tables(count_tok)
    raw_query = projected[:, 0]
    raw_key = projected[:, 1]
    queries = (raw_query * cosine + rotate_half(raw_query) * sine).astype(jnp.bfloat16)
    keys = (raw_key * cosine + rotate_half(raw_key) * sine).astype(jnp.bfloat16)
    values = projected[:, 2].astype(jnp.bfloat16)
    attended, log_totals = attend_forward(queries, keys, values)
    after_attn = stream + jnp.dot(attended, out_weight, preferred_element_type=jnp.float32)
    standard_two, inverse_two = normalize(after_attn)
    normed_ffn = (standard_two * gain_two.astype(jnp.float32)).astype(jnp.bfloat16)
    gate_up = jnp.dot(normed_ffn, in_weight, preferred_element_type=jnp.float32)
    lifted = gate_up[:, :FF]
    gate_part = gate_up[:, FF:]
    normal_cdf = 0.5 * (1.0 + lax.erf(lifted * 0.7071067811865476))
    gelu_value = lifted * normal_cdf
    activated = (gelu_value * gate_part).astype(jnp.bfloat16)
    final = after_attn + jnp.dot(activated, down_weight, preferred_element_type=jnp.float32)
    output = final.astype(jnp.bfloat16)
    gain_one, joint_weight, out_weight = (
        lax.all_gather(gain_attn, "shard", axis=0, tiled=True),
        lax.all_gather(w_qkv, "shard", axis=0, tiled=True),
        lax.all_gather(w_out, "shard", axis=0, tiled=True),
    )
    gain_two, in_weight, down_weight = (
        lax.all_gather(gain_ffn, "shard", axis=0, tiled=True),
        lax.all_gather(w_in, "shard", axis=0, tiled=True),
        lax.all_gather(w_down, "shard", axis=0, tiled=True),
    )
    grad_final = cotangent.astype(jnp.float32)
    grad_down = jnp.einsum("tf,td->fd", activated, cotangent, preferred_element_type=jnp.float32)
    grad_act = jnp.einsum("td,fd->tf", cotangent, down_weight, preferred_element_type=jnp.float32)
    density = jnp.exp(-0.5 * lifted * lifted) * 0.3989422804014327
    grad_lifted = grad_act * gate_part * (normal_cdf + lifted * density)
    grad_gate = grad_act * gelu_value
    grad_gate_up = jnp.concatenate([grad_lifted, grad_gate], axis=1).astype(jnp.bfloat16)
    grad_in = jnp.einsum("td,te->de", normed_ffn, grad_gate_up, preferred_element_type=jnp.float32)
    grad_norm_ffn = jnp.einsum(
        "te,de->td", grad_gate_up, in_weight, preferred_element_type=jnp.float32
    )
    grad_gain_ffn = jnp.sum(grad_norm_ffn * standard_two, axis=0)
    grad_after = grad_final + norm_back(
        grad_norm_ffn, standard_two, inverse_two, gain_two.astype(jnp.float32)
    )
    ffn_members = (grad_gain_ffn, grad_in, grad_down)
    owned_gain_ffn, owned_in, owned_down = (
        lax.psum_scatter(ffn_members[0], "shard", scatter_dimension=0, tiled=True),
        lax.psum_scatter(ffn_members[1], "shard", scatter_dimension=0, tiled=True),
        lax.psum_scatter(ffn_members[2], "shard", scatter_dimension=0, tiled=True),
    )
    grad_branch = grad_after.astype(jnp.bfloat16)
    grad_out = jnp.einsum("td,te->de", attended, grad_branch, preferred_element_type=jnp.float32)
    grad_attended = jnp.einsum(
        "te,de->td", grad_branch, out_weight, preferred_element_type=jnp.float32
    ).astype(jnp.bfloat16)
    grad_query, grad_key, grad_value = attend_backward(
        queries, keys, values, grad_attended, log_totals
    )
    grad_query = grad_query * cosine + rotate_back(grad_query * sine)
    grad_key = grad_key * cosine + rotate_back(grad_key * sine)
    grad_projected = jnp.stack([grad_query, grad_key, grad_value], axis=1)
    grad_projected = grad_projected.reshape(count_tok, 3 * D).astype(jnp.bfloat16)
    grad_qkv = jnp.einsum(
        "td,te->de", normed_attn, grad_projected, preferred_element_type=jnp.float32
    )
    grad_norm_attn = jnp.einsum(
        "te,de->td", grad_projected, joint_weight, preferred_element_type=jnp.float32
    )
    grad_gain_attn = jnp.sum(grad_norm_attn * standard_one, axis=0)
    input_grad = grad_after + norm_back(
        grad_norm_attn, standard_one, inverse_one, gain_one.astype(jnp.float32)
    )
    attn_members = (grad_gain_attn, grad_qkv, grad_out)
    owned_gain_attn, owned_qkv, owned_out = (
        lax.psum_scatter(attn_members[0], "shard", scatter_dimension=0, tiled=True),
        lax.psum_scatter(attn_members[1], "shard", scatter_dimension=0, tiled=True),
        lax.psum_scatter(attn_members[2], "shard", scatter_dimension=0, tiled=True),
    )
    summed = (
        lax.psum(owned_gain_attn.astype(jnp.bfloat16), "replica").astype(jnp.float32),
        lax.psum(owned_qkv.astype(jnp.bfloat16), "replica").astype(jnp.float32),
        lax.psum(owned_out.astype(jnp.bfloat16), "replica").astype(jnp.float32),
        lax.psum(owned_gain_ffn.astype(jnp.bfloat16), "replica").astype(jnp.float32),
        lax.psum(owned_in.astype(jnp.bfloat16), "replica").astype(jnp.float32),
        lax.psum(owned_down.astype(jnp.bfloat16), "replica").astype(jnp.float32),
    )
    return (
        output,
        input_grad.astype(jnp.bfloat16),
        summed[0],
        summed[1],
        summed[2],
        summed[3],
        summed[4],
        summed[5],
    )


def solution(mesh):
    return jax.shard_map(
        body,
        mesh=mesh,
        in_specs=(
            P(("replica", "shard"), None),
            P("shard"),
            P("shard", None),
            P("shard", None),
            P("shard"),
            P("shard", None),
            P("shard", None),
            P(("replica", "shard"), None),
        ),
        out_specs=(
            P(("replica", "shard"), None),
            P(("replica", "shard"), None),
            P("shard"),
            P("shard", None),
            P("shard", None),
            P("shard"),
            P("shard", None),
            P("shard", None),
        ),
        check_vma=False,
    )
```

profile of v0, /device:TPU:0, one launch (start us, length us, event | category | flops | bytes accessed | tf_op | source)
XLA Modules:
  0.0 722.2 jit_solution(9472683614992483625)
XLA Ops:
  14.4 23.5 %all-reduce.13 = (bf16[768]{0:T(1024)(128)(2,1)S(1)}, bf16[768]{0:T(1024)(128)(2,1)S(1)}) all-reduce(bf16[768]{0:T(1024)(128)(2,1)S(1)} %dynamic-update-slice, bf16[768]{0:T(1024)(128)(2,1)S(1)} %dynamic-update-slice.1), channel_id=1, replica_groups=mesh['replica'=4,'shard'=8] {'shard'}, use_global_device_ids=true, to_apply=%add.8 | all-reduce | flops 1536 | bytes 6144
  46.5 31.9 %all-gather.5.cloned.1.call-done = bf16[768,2304]{1,0:T(8,128)(2,1)} async-done(((bf16[96,2304]{1,0:T(8,128)(2,1)}), bf16[768,2304]{1,0:T(8,128)(2,1)}) %all-gather.5.cloned.1.call-update) | async-done | bytes 3538960 | tf_op jit(solution)/shard_map/all_gather | solution.py:184
  78.4 6.0 fusion.96
  112.8 5.6 squeeze.70
  143.6 61.0 %while.30 = (s32[]{:T(128)}, bf16[6,512,4,64]{1,3,2,0:T(8,128)(2,1)}, f32[6,4,512]{2,1,0:T(4,128)}, bf16[6,640,4,64]{1,3,2,0:T(8,128)(2,1)}, s32[6]{0:T(128)S(1)...) while((s32[]{:T(128)}, ...), condition=%wide.region_5.6_spmd, body=%wide.region_2.5_spmd.sunk | while | flops 352716416 | bytes 18297728 | solution.py:131
  214.7 10.7 %fusion.110 = f32[1024,2304]{1,0:T(8,128)} fusion(bf16[768,2304]{1,0:T(8,128)(2,1)} %all-gather.9.cloned.1.call-done, f32[1024,768]{0,1:T(8,128)} %copy-done.4, f32[768]{0:T(1024)S(1)} %convert_element_type.164, f32[1024]{0:T(1024)S(1)} %add_rsqrt_fusion, f32[1024]{0:T(1024)S(1)} %broadcast_multiply_fusion.7), kind=kOutput, calls=%fused_computation.187 | convolution fusion | flops 3627024384 | bytes 16133120 | tf_op jit(solution)/shard_map/dot_general | solution.py:207
  225.4 7.5 %all-gather.11.cloned.1.call-done = bf16[1152,768]{1,0:T(8,128)(2,1)} async-done(((bf16[144,768]{1,0:T(8,128)(2,1)}), bf16[1152,768]{1,0:T(8,128)(2,1)}) %all-gather.11.cloned.1.call-update) | async-done | bytes 1769488 | tf_op jit(solution)/shard_map/all_gather | solution.py:190
  232.8 9.2 %fusion.61 = (bf16[1024,1152]{1,0:T(8,128)(2,1)S(1)}, bf16[1024,1152]{1,0:T(8,128)(2,1)S(1)}, bf16[1024,1152]{1,0:T(8,128)(2,1)}) fusion(f32[1024,2304]{1,0:T(8,128)} %fusion.110, bf16[1024,768]{1,0:T(8,128)(2,1)S(1)} %copy-done.20, bf16[1152,768]{1,0:T(8,128)(2,1)} %all-gather.11.cloned.1.call-done), kind=kOutput, calls=%fused_computation.78 | convolution fusion | flops 1830813696 | bytes 19857408 | tf_op jit(solution)/shard_map/td,fd->tf/dot_general | solution.py:227
  252.6 5.5 fusion.113
  270.5 9.3 %fusion.83 = f32[768,2304]{1,0:T(8,128)} fusion(bf16[1024,1152]{1,0:T(8,128)(2,1)} %copy-done.36, bf16[1024,1152]{1,0:T(8,128)(2,1)} %copy-done.35, f32[1024,768]{0,1:T(8,128)S(1)} %copy-done.6, f32[768]{0:T(1024)S(1)} %convert_element_type.164, f32[1024]{0:T(1024)S(1)} %add_rsqrt_fusion, f32[1024]{0:T(1024)S(1)} %broadcast_multiply_fusion.7), kind=kOutput, calls=%fused_computation.123 | convolution fusion | flops 3636461568 | bytes 14953472 | tf_op jit(solution)/shard_map/td,te->de/dot_general | solution.py:232
  279.8 95.7 %while.31 = (s32[]{:T(128)}, f32[6,512,4,64]{1,3,2,0:T(8,128)}, f32[6,640,4,64]{1,3,2,0:T(8,128)}, f32[6,640,4,64]{1,3,2,0:T(8,128)}, bf16[6,640,4,64]{1,3,2,0:T...) while((s32[]{:T(128)}, f32[6,512,4,64]{1,3,2,0:T(8,128)}, ...), condition=%wide.region_12.13_spmd, body=%wide.region_10.12_spmd.sunk | while | flops 860128896 | bytes 44572060 | solution.py:171
  375.6 5.2 copy.70
  394.9 5.2 copy.71
  411.2 5.6 reshape.526
  420.8 5.6 reshape.532
  426.4 6.0 reshape.531
  445.9 6.2 fusion.94
  452.8 9.3 %fusion.74 = (f32[768]{0:T(1024)S(1)}, f32[1024]{0:T(1024)S(1)}, f32[1024]{0:T(1024)S(1)}, f32[1024,768]{0,1:T(8,128)}) fusion(bf16[1024,768]{0,1:T(8,128)(2,1)S(1)} %copy-done.2, f32[1024]{0:T(1024)S(1)} %copy-done.26, f32[1024]{0:T(1024)S(1)} %copy-done.24, f32[768]{0:T(1024)S(1)} %copy-done.28, bf16[768,2304]{1,0:T(8,128)(2,1)} %all-gather.5.cloned.1.call-done, ...), kind=kOutput, calls=%fused_computation.97 | convolution fusion | flops 3630953728 | bytes 12998656 | tf_op jit(solution)/shard_map/te,de->td/dot_general | solution.py:261
  462.1 20.3 %all-reduce.12 = (bf16[768]{0:T(1024)(128)(2,1)S(1)}, bf16[768]{0:T(1024)(128)(2,1)S(1)}) all-reduce(f32[768]{0:T(1024)S(1)} %get-tuple-element.264, f32[768]{0:T(1024)S(1)} %copy-done.29), channel_id=2, replica_groups=mesh['replica'=4,'shard'=8] {'shard'}, use_global_device_ids=true, to_apply=%region_16.17.clone | all-reduce | flops 1536 | bytes 9216
  482.6 6.2 all-reduce.14
  498.8 36.7 %reduce-scatter.9.cloned.1.call-done = f32[96,2304]{1,0:T(8,128)} async-done(((f32[768,2304]{1,0:T(8,128)}), f32[96,2304]{1,0:T(8,128)}) %reduce-scatter.9.cloned.1.call-update) | async-done | bytes 884752 | tf_op jit(solution)/shard_map/reduce_scatter | solution.py:243
  537.5 130.3 %reduce-scatter.5.cloned.1.call-done = f32[96,2304]{1,0:T(8,128)} async-done(((f32[768,2304]{1,0:T(8,128)}), f32[96,2304]{1,0:T(8,128)}) %reduce-scatter.5.cloned.1.call-update) | async-done | bytes 884752 | tf_op jit(solution)/shard_map/reduce_scatter | solution.py:271
  669.8 5.6 add_convert_fusion
  678.0 31.1 %all-reduce.18.cloned.1.call-done = (bf16[96,2304]{1,0:T(8,128)(2,1)}, bf16[96,768]{1,0:T(8,128)(2,1)}, bf16[96,2304]{1,0:T(8,128)(2,1)}, bf16[144,768]{1,0:T(8,128)(2,1)}) async-done(((bf16[96,2304]{1,0:T(8,128)(2,1)}, bf16[96,768]{1,0:T(8,128)(2,1)}, bf16[96,2304]{1,0:T(8,128)(2,1)}, bf16[144,768]{1,0:T(8,128)(2,1)}), (bf16[96,2304]{1,0:T(8,128)(2,1)}, bf16[96,768]{1,0:T(8,128)(2,1)}, ...) | async-done | bytes 1253392 | tf_op jit(solution)/shard_map/psum | solution.py:276
  (319 shorter events, 315.2 us)
Async XLA Ops:
  7.2 71.2 %all-gather.5.cloned.1.call-start = ((), (), s32[]{:S(2)}) async-start(), calls=%async_computation.4 | async-start | bytes 3981312 | tf_op jit(solution)/shard_map/all_gather | solution.py:184
  7.9 201.3 %all-gather.7.cloned.1.call-start = ((), (), s32[]{:S(2)}) async-start(), calls=%async_computation.5 | async-start | bytes 1327104 | tf_op jit(solution)/shard_map/all_gather | solution.py:185
  8.6 206.0 %all-gather.9.cloned.1.call-start = ((), (), s32[]{:S(2)}) async-start(), calls=%async_computation.6 | async-start | bytes 3981312 | tf_op jit(solution)/shard_map/all_gather | solution.py:189
  9.4 223.4 %all-gather.11.cloned.1.call-start = ((), (), s32[]{:S(2)}) async-start(), calls=%async_computation.7 | async-start | bytes 1990656 | tf_op jit(solution)/shard_map/all_gather | solution.py:190
  10.0 485.3 %reduce-scatter.7.cloned.1.call-start = ((), (), s32[]{:S(2)}) async-start(), calls=%async_computation.9 | async-start | bytes 2654208 | tf_op jit(solution)/shard_map/reduce_scatter | solution.py:272
  11.9 197.4 %copy-start.1 = (bf16[1024,768]{0,1:T(8,128)(2,1)}, bf16[1024,768]{0,1:T(8,128)(2,1)S(1)}, u32[]{:S(2)}) copy-start(bf16[1024,768]{0,1:T(8,128)(2,1)S(1)} %copy.59) | copy-start | bytes 4718596
  12.1 66.2 %copy-start.23 = (f32[1024]{0:T(1024)}, f32[1024]{0:T(1024)S(1)}, u32[]{:S(2)}) copy-start(f32[1024]{0:T(1024)S(1)} %broadcast_multiply_fusion.8) | copy-start | bytes 12292
  12.6 71.7 %copy-start.25 = (f32[1024]{0:T(1024)}, f32[1024]{0:T(1024)S(1)}, u32[]{:S(2)}) copy-start(f32[1024]{0:T(1024)S(1)} %add_rsqrt_fusion.1) | copy-start | bytes 12292
  37.9 46.5 %copy-start.27 = (f32[768]{0:T(1024)}, f32[768]{0:T(1024)S(1)}, u32[]{:S(2)}) copy-start(f32[768]{0:T(1024)S(1)} %convert_element_type.157) | copy-start | bytes 9220
  39.0 51.3 %copy-start.16 = (f32[1024,64]{0,1:T(8,128)}, f32[1024,64]{0,1:T(8,128)S(1)}, u32[]{:S(2)}) copy-start(f32[1024,64]{0,1:T(8,128)S(1)} %get-tuple-element.338) | copy-start | bytes 786436
  39.0 51.3 %copy-start.18 = (f32[1024,64]{0,1:T(8,128)}, f32[1024,64]{0,1:T(8,128)S(1)}, u32[]{:S(2)}) copy-start(f32[1024,64]{0,1:T(8,128)S(1)} %get-tuple-element.339) | copy-start | bytes 786436
  214.7 18.2 %copy-start.20 = (bf16[1024,768]{1,0:T(8,128)(2,1)S(1)}, bf16[1024,768]{1,0:T(8,128)(2,1)}, u32[]{:S(2)}) copy-start(bf16[1024,768]{1,0:T(8,128)(2,1)} %param.19) | copy-start | bytes 4718596
  232.8 9.2 %copy-start.5 = (f32[1024,768]{0,1:T(8,128)S(1)}, f32[1024,768]{0,1:T(8,128)}, u32[]{:S(2)}) copy-start(f32[1024,768]{0,1:T(8,128)} %copy-done.4) | copy-start | bytes 9437188
  232.8 9.2 %copy-start.31 = (bf16[768,2304]{1,0:T(8,128)(2,1)S(1)}, bf16[768,2304]{1,0:T(8,128)(2,1)}, u32[]{:S(2)}) copy-start(bf16[768,2304]{1,0:T(8,128)(2,1)} %all-gather.9.cloned.1.call-done) | copy-start | bytes 10616836
  242.0 4.9 copy-start.35
  242.0 4.9 copy-start.36
  242.1 4.9 copy-start.11
  252.6 244.5 %reduce-scatter.11.cloned.1.call-start = ((), (), s32[]{:S(2)}) async-start(), calls=%async_computation.11 | async-start | bytes 3981312 | tf_op jit(solution)/shard_map/reduce_scatter | solution.py:244
  258.1 277.4 %reduce-scatter.9.cloned.1.call-start = ((), (), s32[]{:S(2)}) async-start(), calls=%async_computation.10 | async-start | bytes 7962624 | tf_op jit(solution)/shard_map/reduce_scatter | solution.py:243
  279.8 388.0 %reduce-scatter.5.cloned.1.call-start = ((), (), s32[]{:S(2)}) async-start(), calls=%async_computation.8 | async-start | bytes 7962624 | tf_op jit(solution)/shard_map/reduce_scatter | solution.py:271
  452.2 256.9 %all-reduce.18.cloned.1.call-start = ((), (), s32[]{:S(2)}) async-start(), calls=%async_computation.12 | async-start | bytes 2506752 | tf_op jit(solution)/shard_map/psum | solution.py:276
  452.8 9.3 %copy-start.29 = (f32[768]{0:T(1024)S(1)}, f32[768]{0:T(1024)}, u32[]{:S(2)}) copy-start(f32[768]{0:T(1024)} %get-tuple-element.262) | copy-start | bytes 9220
  495.3 174.5 %copy-start.7 = (f32[1024,768]{0,1:T(8,128)S(1)}, f32[1024,768]{0,1:T(8,128)}, u32[]{:S(2)}) copy-start(f32[1024,768]{0,1:T(8,128)} %copy-done.4) | copy-start | bytes 9437188
  709.0 5.7 copy-start.22
  (23 other events, 64.5 us)
Sparse Core Ops, SparseCore 0:
  10.2 68.1 all-gather.4
  80.5 39.5 all-gather.6
  122.3 63.9 all-gather.8
  188.3 44.4 all-gather.10
  252.7 68.0 reduce-scatter.6
  324.2 78.1 reduce-scatter.10
  406.1 129.3 reduce-scatter.8
  539.6 128.0 reduce-scatter.4
  671.0 38.0 all-reduce.17
where the time goes:
time: 734 us; the launch traced here: 722 us
  waiting for transfers between devices  240 us (33%)
  matrix products  179 us (24%)
  local copies, waits for them, and re-layouts  142 us (19%)
  other arithmetic  86 us (12%)
  blocking collectives  50 us (7%)
  between operations  16 us (2%)
  loops' own time  8.62 us (1%)
    reduce_scatter x1, waiting for transfers between devices, body(): lax.psum_scatter(attn_members[1], 'shard', scatter_dimension=0, tiled=True)  130 us
    unnamed x2, blocking collectives  43.8 us
    reduce_scatter x1, waiting for transfers between devices, body(): lax.psum_scatter(ffn_members[1], 'shard', scatter_dimension=0, tiled=True)  36.7 us
    all_gather x1, waiting for transfers between devices, body(): lax.all_gather(w_qkv, 'shard', axis=0, tiled=True)  31.9 us
    psum x1, waiting for transfers between devices, body(): lax.psum(owned_qkv.astype(jnp.bfloat16), 'replica').astype(jnp.float32)  31.1 us
    dot_general x12, matrix products, block_scores(): jnp.einsum('qhd,khd->hqk', query_part, key_part, preferred_element_type=j...  24.6 us
    unnamed x86, local copies, waits for them, and re-layouts  21.1 us
    dot_general x6, matrix products, one_block(): jnp.einsum('hqk,khd->qhd', probs, value_part, preferred_element_type=jnp....  20.8 us
  transfers between devices with their start and end apart: 9, of which 5 were waited for; matrix products, arithmetic and copies ran while one was open for 51% of the time, Pallas kernels for 0%

commit v1 on v0

--- a/solution.py
+++ b/solution.py
@@ -11,6 +11,19 @@
 WINDOW = 128
 LENGTH = 1024
 epsilon = 1e-05
+
+
+def ring_gather(x, axis, dim):
+    ways = lax.axis_size(axis)
+    up = [(d, (d + 1) % ways) for d in range(ways)]
+    down = [(d, (d - 1) % ways) for d in range(ways)]
+    earlier, later = ([x], [x])
+    for _ in range(ways // 2):
+        earlier.append(lax.ppermute(earlier[-1], axis, up))
+    for _ in range((ways - 1) // 2):
+        later.append(lax.ppermute(later[-1], axis, down))
+    line = jnp.concatenate([*earlier[::-1], *later[1:]], axis=dim)
+    return jnp.roll(line, (lax.axis_index(axis) - ways // 2) * x.shape[dim], axis=dim)
 
 
 def normalize(values):
@@ -181,7 +194,7 @@
     count_tok = tokens.shape[0]
     gain_one, joint_weight, out_weight = (
         lax.all_gather(gain_attn, "shard", axis=0, tiled=True),
-        lax.all_gather(w_qkv, "shard", axis=0, tiled=True),
+        ring_gather(w_qkv, "shard", 0),
         lax.all_gather(w_out, "shard", axis=0, tiled=True),
     )
     gain_two, in_weight, down_weight = (

time: 734 us -> 757 us (1.031)
  starting transfers between devices: 0.36 us -> 16.6 us
  waiting for transfers between devices: 240 us -> 248 us
    ppermute x0 -> x7, waiting for transfers between devices: none -> 46.6 us  [the longest x4 24.6 us: ring_gather(): earlier.append(lax.ppermute(earlier[-1], axis, up))]
    all_gather x1, waiting for transfers between devices: 31.9 us -> 0.02 us  [body(): lax.all_gather(w_qkv, 'shard', axis=0, tiled=True)]
    ppermute x0 -> x7, starting transfers between devices: none -> 16.3 us  [the longest x3 10 us: ring_gather(): later.append(lax.ppermute(later[-1], axis, down))]
    unnamed x86 -> x103, local copies, waits for them, and re-layouts: 21.1 us -> 23.3 us
  transfers between devices with their start and end apart: 9 -> 16, of which waited for: 5 -> 7; matrix products, arithmetic and copies ran while one was open for 51% -> 52% of each run, Pallas kernels for 0% -> 0%
where the time goes in v1:
time: 757 us; the launch traced here: 750 us
  waiting for transfers between devices  248 us (33%)
  matrix products  178 us (24%)
  local copies, waits for them, and re-layouts  144 us (19%)
  other arithmetic  85.9 us (11%)
  blocking collectives  53.2 us (7%)
  starting transfers between devices  16.6 us (2%)
  between operations  16.1 us (2%)
  loops' own time  8.46 us (1%)
    reduce_scatter x1, waiting for transfers between devices, body(): lax.psum_scatter(attn_members[1], 'shard', scatter_dimension=0, tiled=True)  130 us
    unnamed x2, blocking collectives  47 us
    reduce_scatter x1, waiting for transfers between devices, body(): lax.psum_scatter(ffn_members[1], 'shard', scatter_dimension=0, tiled=True)  38.1 us
    psum x1, waiting for transfers between devices, body(): lax.psum(owned_qkv.astype(jnp.bfloat16), 'replica').astype(jnp.float32)  31.1 us
    dot_general x12, matrix products, block_scores(): jnp.einsum('qhd,khd->hqk', query_part, key_part, preferred_element_type=j...  24.6 us
    ppermute x4, waiting for transfers between devices, ring_gather(): earlier.append(lax.ppermute(earlier[-1], axis, up))  24.6 us
    unnamed x103, local copies, waits for them, and re-layouts  23.3 us
    ppermute x3, waiting for transfers between devices, ring_gather(): later.append(lax.ppermute(later[-1], axis, down))  22 us
  transfers between devices with their start and end apart: 16, of which 7 were waited for; matrix products, arithmetic and copies ran while one was open for 52% of the time, Pallas kernels for 0%

profile of v1, /device:TPU:0, one launch (start us, length us, event | category | flops | bytes accessed | tf_op | source)
XLA Modules:
  0.0 749.9 jit_solution(902008537166593724)
XLA Ops:
  16.8 16.5 %collective-permute-done = bf16[96,2304]{1,0:T(8,128)(2,1)S(1)} collective-permute-done((bf16[96,2304]{1,0:T(8,128)(2,1)}, bf16[96,2304]{1,0:T(8,128)(2,1)S(1)}, u32[]{:S(2)}, u32[]{:S(2)}) %collective-permute-start) | collective-permute-done | bytes 442400 | tf_op jit(solution)/shard_map/ppermute | solution.py:22
  40.2 8.0 %collective-permute-done.1 = bf16[96,2304]{1,0:T(8,128)(2,1)S(1)} collective-permute-done((bf16[96,2304]{1,0:T(8,128)(2,1)S(1)}, bf16[96,2304]{1,0:T(8,128)(2,1)S(1)}, u32[]{:S(2)}, u32[]{:S(2)}) %collective-permute-start.1) | collective-permute-done | bytes 442400 | tf_op jit(solution)/shard_map/ppermute | solution.py:22
  52.6 23.9 %all-reduce.13 = (bf16[768]{0:T(1024)(128)(2,1)S(1)}, bf16[768]{0:T(1024)(128)(2,1)S(1)}) all-reduce(bf16[768]{0:T(1024)(128)(2,1)S(1)} %dynamic-update-slice, bf16[768]{0:T(1024)(128)(2,1)S(1)} %dynamic-update-slice.1), channel_id=1, replica_groups=mesh['replica'=4,'shard'=8] {'shard'}, use_global_device_ids=true, to_apply=%add.8 | all-reduce | flops 1536 | bytes 6144
  82.4 17.1 %collective-permute-done.5 = bf16[96,2304]{1,0:T(8,128)(2,1)S(1)} collective-permute-done((bf16[96,2304]{1,0:T(8,128)(2,1)S(1)}, bf16[96,2304]{1,0:T(8,128)(2,1)S(1)}, u32[]{:S(2)}, u32[]{:S(2)}) %collective-permute-start.5) | collective-permute-done | bytes 442400 | tf_op jit(solution)/shard_map/ppermute | solution.py:24
  144.6 5.6 squeeze.70
  174.9 60.9 %while.30 = (s32[]{:T(128)}, bf16[6,512,4,64]{1,3,2,0:T(8,128)(2,1)}, f32[6,4,512]{2,1,0:T(4,128)}, bf16[6,640,4,64]{1,3,2,0:T(8,128)(2,1)}, s32[6]{0:T(128)S(1)...) while((s32[]{:T(128)}, ...), condition=%wide.region_5.6_spmd, body=%wide.region_2.5_spmd.sunk | while | flops 352716416 | bytes 18297728 | solution.py:144
  245.8 10.7 %fusion.112 = f32[1024,2304]{1,0:T(8,128)} fusion(bf16[768,2304]{1,0:T(8,128)(2,1)} %all-gather.7.cloned.1.call-done, f32[1024,768]{0,1:T(8,128)} %copy-done.4, f32[768]{0:T(1024)S(1)} %convert_element_type.164, f32[1024]{0:T(1024)S(1)} %add_rsqrt_fusion, f32[1024]{0:T(1024)S(1)} %broadcast_multiply_fusion.7), kind=kOutput, calls=%fused_computation.205 | convolution fusion | flops 3627024384 | bytes 16133120 | tf_op jit(solution)/shard_map/dot_general | solution.py:220
  256.5 9.2 %fusion.61 = (bf16[1024,1152]{1,0:T(8,128)(2,1)S(1)}, bf16[1024,1152]{1,0:T(8,128)(2,1)S(1)}, bf16[1024,1152]{1,0:T(8,128)(2,1)}) fusion(f32[1024,2304]{1,0:T(8,128)} %fusion.112, bf16[1024,768]{1,0:T(8,128)(2,1)S(1)} %copy-done.21, bf16[1152,768]{1,0:T(8,128)(2,1)} %all-gather.9.cloned.1.call-done), kind=kOutput, calls=%fused_computation.78 | convolution fusion | flops 1830813696 | bytes 19857408 | tf_op jit(solution)/shard_map/td,fd->tf/dot_general | solution.py:240
  276.4 5.5 fusion.115
  294.1 9.3 %fusion.85 = f32[768,2304]{1,0:T(8,128)} fusion(bf16[1024,1152]{1,0:T(8,128)(2,1)} %copy-done.37, bf16[1024,1152]{1,0:T(8,128)(2,1)} %copy-done.36, f32[1024,768]{0,1:T(8,128)S(1)} %copy-done.6, f32[768]{0:T(1024)S(1)} %convert_element_type.164, f32[1024]{0:T(1024)S(1)} %add_rsqrt_fusion, f32[1024]{0:T(1024)S(1)} %broadcast_multiply_fusion.7), kind=kOutput, calls=%fused_computation.125 | convolution fusion | flops 3636461568 | bytes 14953472 | tf_op jit(solution)/shard_map/td,te->de/dot_general | solution.py:245
  303.4 95.7 %while.31 = (s32[]{:T(128)}, f32[6,512,4,64]{1,3,2,0:T(8,128)}, f32[6,640,4,64]{1,3,2,0:T(8,128)}, f32[6,640,4,64]{1,3,2,0:T(8,128)}, bf16[6,640,4,64]{1,3,2,0:T...) while((s32[]{:T(128)}, f32[6,512,4,64]{1,3,2,0:T(8,128)}, ...), condition=%wide.region_12.13_spmd, body=%wide.region_10.12_spmd.sunk | while | flops 860128896 | bytes 44572060 | solution.py:184
  399.1 5.2 copy.70
  418.3 5.2 copy.71
  434.6 5.6 reshape.526
  444.3 5.7 reshape.532
  450.0 6.0 reshape.531
  469.5 6.2 fusion.96
  476.4 9.3 %fusion.76 = (f32[768]{0:T(1024)S(1)}, f32[1024]{0:T(1024)S(1)}, f32[1024]{0:T(1024)S(1)}, f32[1024,768]{0,1:T(8,128)}) fusion(bf16[1024,768]{0,1:T(8,128)(2,1)S(1)} %copy-done.2, f32[1024]{0:T(1024)S(1)} %copy-done.29, f32[1024]{0:T(1024)S(1)} %copy-done.25, f32[768]{0:T(1024)S(1)} %copy-done.27, bf16[768,2304]{1,0:T(8,128)(2,1)} %all-gather.11.cloned.1.call-done, ...), kind=kOutput, calls=%fused_computation.99 | convolution fusion | flops 3630953728 | bytes 12998656 | tf_op jit(solution)/shard_map/te,de->td/dot_general | solution.py:274
  485.7 23.0 %all-reduce.12 = (bf16[768]{0:T(1024)(128)(2,1)S(1)}, bf16[768]{0:T(1024)(128)(2,1)S(1)}) all-reduce(f32[768]{0:T(1024)S(1)} %get-tuple-element.264, f32[768]{0:T(1024)S(1)} %copy-done.30), channel_id=2, replica_groups=mesh['replica'=4,'shard'=8] {'shard'}, use_global_device_ids=true, to_apply=%region_16.17.clone | all-reduce | flops 1536 | bytes 9216
  508.9 6.2 all-reduce.14
  525.1 38.1 %reduce-scatter.9.cloned.1.call-done = f32[96,2304]{1,0:T(8,128)} async-done(((f32[768,2304]{1,0:T(8,128)}), f32[96,2304]{1,0:T(8,128)}) %reduce-scatter.9.cloned.1.call-update) | async-done | bytes 884752 | tf_op jit(solution)/shard_map/reduce_scatter | solution.py:256
  565.2 130.2 %reduce-scatter.5.cloned.1.call-done = f32[96,2304]{1,0:T(8,128)} async-done(((f32[768,2304]{1,0:T(8,128)}), f32[96,2304]{1,0:T(8,128)}) %reduce-scatter.5.cloned.1.call-update) | async-done | bytes 884752 | tf_op jit(solution)/shard_map/reduce_scatter | solution.py:284
  697.4 5.6 add_convert_fusion
  705.6 31.1 %all-reduce.18.cloned.1.call-done = (bf16[96,2304]{1,0:T(8,128)(2,1)}, bf16[96,768]{1,0:T(8,128)(2,1)}, bf16[96,2304]{1,0:T(8,128)(2,1)}, bf16[144,768]{1,0:T(8,128)(2,1)}) async-done(((bf16[96,2304]{1,0:T(8,128)(2,1)}, bf16[96,768]{1,0:T(8,128)(2,1)}, bf16[96,2304]{1,0:T(8,128)(2,1)}, bf16[144,768]{1,0:T(8,128)(2,1)}), (bf16[96,2304]{1,0:T(8,128)(2,1)}, bf16[96,768]{1,0:T(8,128)(2,1)}, ...) | async-done | bytes 1253392 | tf_op jit(solution)/shard_map/psum | solution.py:289
  (351 shorter events, 342.2 us)
Async XLA Ops:
  7.2 43.6 %copy-start.31 = (u32[32]{0:T(128)S(1)}, u32[32]{0:T(128)}, u32[]{:S(2)}) copy-start(u32[32]{0:T(128)} %constant.236) | copy-start | bytes 388
  7.2 44.9 %copy-start.34 = (bf16[96]{0:T(256)(128)(2,1)S(1)}, bf16[96]{0:T(256)(128)(2,1)}, u32[]{:S(2)}) copy-start(bf16[96]{0:T(256)(128)(2,1)} %param.13) | copy-start | bytes 580
  7.2 45.2 %copy-start.35 = (bf16[96]{0:T(256)(128)(2,1)S(1)}, bf16[96]{0:T(256)(128)(2,1)}, u32[]{:S(2)}) copy-start(bf16[96]{0:T(256)(128)(2,1)} %param.16) | copy-start | bytes 580
  7.2 233.2 %all-gather.5.cloned.1.call-start = ((), (), s32[]{:S(2)}) async-start(), calls=%async_computation.4 | async-start | bytes 1327104 | tf_op jit(solution)/shard_map/all_gather | solution.py:198
  7.9 237.9 %all-gather.7.cloned.1.call-start = ((), (), s32[]{:S(2)}) async-start(), calls=%async_computation.5 | async-start | bytes 3981312 | tf_op jit(solution)/shard_map/all_gather | solution.py:202
  8.7 247.8 %all-gather.9.cloned.1.call-start = ((), (), s32[]{:S(2)}) async-start(), calls=%async_computation.6 | async-start | bytes 1990656 | tf_op jit(solution)/shard_map/all_gather | solution.py:203
  9.4 467.0 %all-gather.11.cloned.1.call-start = ((), (), s32[]{:S(2)}) async-start(), calls=%async_computation.7 | async-start | bytes 3981312 | tf_op jit(solution)/shard_map/all_gather | solution.py:230
  9.5 23.8 %collective-permute-start = (bf16[96,2304]{1,0:T(8,128)(2,1)}, bf16[96,2304]{1,0:T(8,128)(2,1)S(1)}, u32[]{:S(2)}, u32[]{:S(2)}) collective-permute-start(bf16[96,2304]{1,0:T(8,128)(2,1)} %param.14), channel_id=1, source_target_pairs={{0,1},{1,2},{2,3},{3,4},{4,5},{5,6},{6,7},{7,0},{8,9},{9,10},{10,1... | collective-permute-start | bytes 1327112 | tf_op jit(solution)/shard_map/ppermute | solution.py:22
  12.5 67.1 %collective-permute-start.4 = (bf16[96,2304]{1,0:T(8,128)(2,1)}, bf16[96,2304]{1,0:T(8,128)(2,1)S(1)}, u32[]{:S(2)}, u32[]{:S(2)}) collective-permute-start(bf16[96,2304]{1,0:T(8,128)(2,1)} %param.14), channel_id=1, source_target_pairs={{0,7},{1,0},{2,1},{3,2},{4,3},{5,4},{6,5},{7,6},{8,15},{9,8},{10,9... | collective-permute-start | bytes 1327112 | tf_op jit(solution)/shard_map/ppermute | solution.py:24
  15.6 505.9 %reduce-scatter.7.cloned.1.call-start = ((), (), s32[]{:S(2)}) async-start(), calls=%async_computation.9 | async-start | bytes 2654208 | tf_op jit(solution)/shard_map/reduce_scatter | solution.py:285
  16.8 104.9 %copy-start.17 = (f32[1024,64]{0,1:T(8,128)}, f32[1024,64]{0,1:T(8,128)S(1)}, u32[]{:S(2)}) copy-start(f32[1024,64]{0,1:T(8,128)S(1)} %get-tuple-element.338) | copy-start | bytes 786436
  16.8 104.9 %copy-start.19 = (f32[1024,64]{0,1:T(8,128)}, f32[1024,64]{0,1:T(8,128)S(1)}, u32[]{:S(2)}) copy-start(f32[1024,64]{0,1:T(8,128)S(1)} %get-tuple-element.339) | copy-start | bytes 786436
  33.3 14.9 %collective-permute-start.1 = (bf16[96,2304]{1,0:T(8,128)(2,1)S(1)}, bf16[96,2304]{1,0:T(8,128)(2,1)S(1)}, u32[]{:S(2)}, u32[]{:S(2)}) collective-permute-start(bf16[96,2304]{1,0:T(8,128)(2,1)S(1)} %collective-permute-done), channel_id=1, source_target_pairs={{0,1},{1,2},{2,3},{3,4},{4,5},{5,6},{6,7},{7,0},{8,9},{9,10},{10,1... | collective-permute-start | bytes 1327112 | tf_op jit(solution)/shard_map/ppermute | solution.py:22
  48.2 33.7 %collective-permute-start.2 = (bf16[96,2304]{1,0:T(8,128)(2,1)S(1)}, bf16[96,2304]{1,0:T(8,128)(2,1)}, u32[]{:S(2)}, u32[]{:S(2)}) collective-permute-start(bf16[96,2304]{1,0:T(8,128)(2,1)S(1)} %collective-permute-done.1), channel_id=1, source_target_pairs={{0,1},{1,2},{2,3},{3,4},{4,5},{5,6},{6,7},{7,0},{8,9},{9,10},{10,1... | collective-permute-start | bytes 1327112 | tf_op jit(solution)/shard_map/ppermute | solution.py:22
  50.7 189.7 %copy-start.1 = (bf16[1024,768]{0,1:T(8,128)(2,1)}, bf16[1024,768]{0,1:T(8,128)(2,1)S(1)}, u32[]{:S(2)}) copy-start(bf16[1024,768]{0,1:T(8,128)(2,1)S(1)} %copy.59) | copy-start | bytes 4718596
  76.5 35.2 %copy-start.26 = (f32[768]{0:T(1024)}, f32[768]{0:T(1024)S(1)}, u32[]{:S(2)}) copy-start(f32[768]{0:T(1024)S(1)} %convert_element_type.157) | copy-start | bytes 9220
  79.6 20.0 %collective-permute-start.5 = (bf16[96,2304]{1,0:T(8,128)(2,1)S(1)}, bf16[96,2304]{1,0:T(8,128)(2,1)S(1)}, u32[]{:S(2)}, u32[]{:S(2)}) collective-permute-start(bf16[96,2304]{1,0:T(8,128)(2,1)S(1)} %collective-permute-done.4), channel_id=1, source_target_pairs={{0,7},{1,0},{2,1},{3,2},{4,3},{5,4},{6,5},{7,6},{8,15},{9,8},{10,9... | collective-permute-start | bytes 1327112 | tf_op jit(solution)/shard_map/ppermute | solution.py:24
  81.9 22.2 %collective-permute-start.3 = (bf16[96,2304]{1,0:T(8,128)(2,1)}, bf16[96,2304]{1,0:T(8,128)(2,1)S(1)}, u32[]{:S(2)}, u32[]{:S(2)}) collective-permute-start(bf16[96,2304]{1,0:T(8,128)(2,1)} %collective-permute-done.2), channel_id=1, source_target_pairs={{0,1},{1,2},{2,3},{3,4},{4,5},{5,6},{6,7},{7,0},{8,9},{9,10},{10,1... | collective-permute-start | bytes 1327112 | tf_op jit(solution)/shard_map/ppermute | solution.py:22
  99.5 10.8 %collective-permute-start.6 = (bf16[96,2304]{1,0:T(8,128)(2,1)S(1)}, bf16[96,2304]{1,0:T(8,128)(2,1)S(1)}, u32[]{:S(2)}, u32[]{:S(2)}) collective-permute-start(bf16[96,2304]{1,0:T(8,128)(2,1)S(1)} %collective-permute-done.5), channel_id=1, source_target_pairs={{0,7},{1,0},{2,1},{3,2},{4,3},{5,4},{6,5},{7,6},{8,15},{9,8},{10,9... | collective-permute-start | bytes 1327112 | tf_op jit(solution)/shard_map/ppermute | solution.py:24
  276.3 247.0 %reduce-scatter.11.cloned.1.call-start = ((), (), s32[]{:S(2)}) async-start(), calls=%async_computation.11 | async-start | bytes 3981312 | tf_op jit(solution)/shard_map/reduce_scatter | solution.py:257
  281.9 281.3 %reduce-scatter.9.cloned.1.call-start = ((), (), s32[]{:S(2)}) async-start(), calls=%async_computation.10 | async-start | bytes 7962624 | tf_op jit(solution)/shard_map/reduce_scatter | solution.py:256
  303.4 392.0 %reduce-scatter.5.cloned.1.call-start = ((), (), s32[]{:S(2)}) async-start(), calls=%async_computation.8 | async-start | bytes 7962624 | tf_op jit(solution)/shard_map/reduce_scatter | solution.py:284
  475.7 261.0 %all-reduce.18.cloned.1.call-start = ((), (), s32[]{:S(2)}) async-start(), calls=%async_computation.12 | async-start | bytes 2506752 | tf_op jit(solution)/shard_map/psum | solution.py:289
  521.6 175.8 %copy-start.7 = (f32[1024,768]{0,1:T(8,128)S(1)}, f32[1024,768]{0,1:T(8,128)}, u32[]{:S(2)}) copy-start(f32[1024,768]{0,1:T(8,128)} %copy-done.4) | copy-start | bytes 9437188
  (31 other events, 200.1 us)
Sparse Core Ops, SparseCore 0:
  10.2 53.4 all-gather.4
  65.9 84.3 all-gather.6
  152.5 44.4 all-gather.8
  199.0 64.1 all-gather.10
  276.5 71.9 reduce-scatter.6
  351.9 78.1 reduce-scatter.10
  433.8 129.3 reduce-scatter.8
  567.3 128.0 reduce-scatter.4
  698.6 38.0 all-reduce.17
